TPU v7x, 32 devices: a whole 2x2x4 slice. The times are simulated.
32 devices in a mesh: blocks: 2 (over x), slab: 16 (over z, y, core).
Axes of the slice: x: 2, y: 2, z: 4, core: 2. Of those that a mesh axis runs over, the one named last changes fastest.
Arguments:
- estimate: float32 [64, 256, 128], P('blocks', 'slab'), parts along dimension 0, may hold values from 0.25 to 8, as said below
- raw_views: float32 [6, 64, 256, 128], P(None, 'blocks', 'slab'), parts along dimension 1, may hold values from 0.1 to 30, as said below
- psf_taps: float32 [6, 3, 31], replicated, may hold values from 0 to 1, as said below
Outputs:
- restored: float32 [64, 256, 128], P('blocks', 'slab'), parts along dimension 0
There are 2 independent parts, one for each index of `blocks`. A program takes and returns all parts, laid end to end along the dimension named above; an argument that names none is the same for every part. Nothing has to cross between parts.
Inputs may be any that keep to these rules, and one draw needn't show every extreme that they name: `estimate`: positive. `raw_views`: positive. `psf_taps`: every tap is positive, and each view's taps along each dimension sum to 1.
All inputs are finite; a program needn't handle non-finite values.
Results may differ from a plain program's by a relative error of at most 0.0001.
Values sent between devices are 32-bit elements; how exact they have to be, the bound alone decides.
A program may use at most 64 MiB of HBM per device.

v0:
```python
import jax
import jax.numpy as jnp
from jax import lax
from jax.experimental import pallas as pl
from jax.experimental.pallas import tpu as pltpu
from jax.sharding import PartitionSpec as P

ITERS = 2
F32 = jnp.float32
BF16 = jnp.bfloat16
MESH = pl.DeviceIdType.MESH


def split(x):
    hi = x.astype(BF16)
    return hi, (x - hi.astype(F32)).astype(BF16)


def dot(a, b):
    return jnp.dot(a, b, preferred_element_type=F32)


def iota(shape, dim):
    return lax.broadcasted_iota(jnp.int32, shape, dim)


def build_matrices(v, tap_pad, ay, ayt, wx, mz):
    near = jnp.abs(iota((128, 128), 0) - iota((128, 128), 1)) <= 15

    def band(d):
        row = jnp.broadcast_to(tap_pad[v, pl.ds(d, 1), :], (128, 128))
        return jnp.where(near, pltpu.roll(row, 113, 1, stride=1, stride_axis=0), 0.0)

    def placed(block, width):
        hi, lo = (p.astype(F32) for p in split(block))
        zero = jnp.zeros_like(hi)
        hi, lo = jnp.concatenate([hi, zero], 1), jnp.concatenate([lo, zero], 1)
        return (hi + pltpu.roll(hi, width, 1) + pltpu.roll(lo, 2 * width, 1)).astype(BF16)

    ty = band(1)
    ay[pl.ds(pl.multiple_of(v * 48, 16), 48), :] = placed(ty[16:64], 80)
    ayt[v] = placed(ty.T[16:32], 48)[:, :144]

    tx = band(2)
    for direction, w in ((0, tx.T), (1, tx)):
        hi, lo = split(w)
        wx[direction, v, 0:128, 0:128] = hi
        wx[direction, v, 128:256, 0:128] = hi
        wx[direction, v, 0:128, 128:256] = lo
        wx[direction, v, 128:256, 128:256] = jnp.zeros_like(hi)

    tz = band(0)
    spread = (iota((256, 128), 0) // 8 == iota((256, 128), 1)).astype(F32).astype(BF16)
    spread_t = (iota((128, 256), 0) == iota((128, 256), 1) // 8).astype(F32).astype(BF16)
    same = (iota((256, 256), 0) % 8) == (iota((256, 256), 1) % 8)
    for direction, m in ((0, tz), (1, tz.T)):
        for half, part in enumerate(split(m)):
            wide = dot(dot(spread, part).astype(BF16), spread_t)
            mz[direction, v, 256 * half : 256 * half + 256, :] = jnp.where(same, wide, 0.0).astype(BF16)


def columns_then_planes(pair, w, m):
    r = dot(pair, w)
    rhs = jnp.concatenate(split(r[:, :128] + r[:, 128:]), 1)
    q = dot(m, rhs)
    return (q[:256, :128] + q[:256, 128:]) + (q[256:, :128] + q[256:, 128:])


def kernel(
    n, views,
    est, raw, taps, out,
    tap_pad, ay, ayt, wx, mz, halo, raw_halo, frame, g_pair, ratio3, k_pair, acc, cur, stat, msg, msgs,
    est_send, est_recv, raw_send, raw_recv, msg_send, msg_recv,
):
    me = lax.axis_index("slab")
    has_left, has_right = me > 0, me < n - 1
    left, right = lax.rem(me + n - 1, n), lax.rem(me + 1, n)

    barrier = pltpu.get_barrier_semaphore()

    def greet(d, _):
        pl.semaphore_signal(barrier, inc=1, device_id={"slab": lax.rem(me + d, n)}, device_id_type=MESH)
        return 0

    lax.fori_loop(1, n, greet, 0)
    pl.semaphore_wait(barrier, n - 1)

    def copy(src, dst, send, recv, to):
        return pltpu.make_async_remote_copy(
            src_ref=src, dst_ref=dst, send_sem=send, recv_sem=recv, device_id={"slab": to}, device_id_type=MESH
        )

    def est_copies(it, source):
        srcs = (source, source, halo.at[it, 0], halo.at[it, 1])
        tos = (right, left, right, left)
        return [
            copy(srcs[k], halo.at[it, k], est_send.at[it, k], est_recv.at[it, k], tos[k]) for k in range(4)
        ]

    both = has_left & has_right
    sends = (has_right, has_left, both, both)
    recvs = (has_left, has_right, me > 1, me < n - 2)

    def raw_copy(v, k):
        return copy(raw.at[v], raw_halo.at[k, v], raw_send.at[v, k], raw_recv.at[v, k], (right, left)[k])

    first = est_copies(0, est)
    pl.when(has_right)(first[0].start)
    pl.when(has_left)(first[1].start)

    tap_pad[...] = jnp.zeros_like(tap_pad)
    for v in range(views):
        tap_pad[v, 0:3, 0:31] = taps[v]
    stat[...] = jnp.zeros_like(stat)
    frame[:, 240:256, :] = jnp.zeros((32, 16, 128), BF16)
    for it in range(ITERS):
        for k, there in enumerate(recvs):
            @pl.when(jnp.logical_not(there))
            def _():
                halo[it, k] = jnp.zeros((32, 16, 128), F32)

    def put_block(b, ref_block):
        hi, lo = split(ref_block[...])
        frame[:, 16 * b : 16 * b + 16, :] = hi
        frame[:, 80 + 16 * b : 96 + 16 * b, :] = lo
        frame[:, 160 + 16 * b : 176 + 16 * b, :] = hi

    def exchange(it, copies, source, meanwhile):
        put_block(2, source)
        for k in (0, 1):
            pl.when(recvs[k])(copies[k].wait_recv)
            pl.when(sends[2 + k])(copies[2 + k].start)
        meanwhile()
        put_block(1, halo.at[it, 0])
        put_block(3, halo.at[it, 1])
        for k in (2, 3):
            pl.when(recvs[k])(copies[k].wait_recv)
        put_block(0, halo.at[it, 2])
        put_block(4, halo.at[it, 3])

    def start_raw():
        def go(v, _):
            pl.when(has_right)(raw_copy(v, 0).start)
            pl.when(has_left)(raw_copy(v, 1).start)
            return 0

        lax.fori_loop(0, views, go, 0)

        def build(v, _):
            build_matrices(v, tap_pad, ay, ayt, wx, mz)
            return 0

        lax.fori_loop(0, views, build, 0)

    def rows_forward():
        def step(k, _):
            rhs = jnp.concatenate([frame[2 * k], frame[2 * k + 1]], 1)
            rows = pl.ds(pl.multiple_of(16 * k, 16), 16)
            for v in range(views):
                res = dot(ay[48 * v : 48 * v + 48, :], rhs)
                for t in range(6):
                    two = jnp.concatenate([res[8 * t : 8 * t + 8, :128], res[8 * t : 8 * t + 8, 128:]], 0)
                    hi, lo = split(two)
                    g_pair[v, t, rows, 0:128] = hi
                    g_pair[v, t, rows, 128:256] = lo
            return 0

        lax.fori_loop(0, 16, step, 0)

    def blur_and_ratio(it, v):
        w, m = wx[0, v], mz[0, v]
        blurred = [columns_then_planes(g_pair[v, t], w, m).reshape(32, 8, 128) for t in range(6)]
        total = jnp.sum(blurred[2] + blurred[3], axis=0)
        stat[2 * it, pl.ds(v, 1), :] = jnp.sum(total, axis=0, keepdims=True)
        if it == 0:
            counts = jnp.sum(raw[v, :, 0:8, :] + raw[v, :, 8:16, :], axis=0)
            stat[1, pl.ds(v, 1), :] = jnp.sum(counts, axis=0, keepdims=True)
            pl.when(has_left)(raw_copy(v, 0).wait_recv)
            pl.when(has_right)(raw_copy(v, 1).wait_recv)
        for b, (block, there) in enumerate(
            ((raw_halo.at[0, v], has_left), (raw.at[v], None), (raw_halo.at[1, v], has_right))
        ):
            value = block[...] / jnp.concatenate([blurred[2 * b], blurred[2 * b + 1]], 1)
            if there is not None:
                value = jnp.where(there, value, 0.0)
            hi, lo = split(value)
            ratio3[v, :, 16 * b : 16 * b + 16, :] = hi
            ratio3[v, :, 48 + 16 * b : 64 + 16 * b, :] = lo
            ratio3[v, :, 96 + 16 * b : 112 + 16 * b, :] = hi

    def adjoint_log(v):
        a = ayt[v]
        for k in range(16):
            res = dot(a, jnp.concatenate([ratio3[v, 2 * k], ratio3[v, 2 * k + 1]], 1))
            for t in range(2):
                two = jnp.concatenate([res[8 * t : 8 * t + 8, :128], res[8 * t : 8 * t + 8, 128:]], 0)
                hi, lo = split(two)
                k_pair[t, 16 * k : 16 * k + 16, 0:128] = hi
                k_pair[t, 16 * k : 16 * k + 16, 128:256] = lo
        w, m = wx[1, v], mz[1, v]
        for t in range(2):
            acc[t] += jnp.log(columns_then_planes(k_pair[t], w, m))

    def msg_copy(d):
        return copy(msg, msgs.at[d], msg_send.at[d], msg_recv.at[d], lax.rem(me + d, n))

    exchange(0, first, est, start_raw)
    rows_forward()
    acc[...] = jnp.zeros_like(acc)

    def view0(v, _):
        blur_and_ratio(0, v)
        adjoint_log(v)
        return 0

    lax.fori_loop(0, views, view0, 0)
    for t in range(2):
        cur[:, 8 * t : 8 * t + 8, :] = est[:, 8 * t : 8 * t + 8, :] * jnp.exp(
            acc[t] * (1.0 / views)
        ).reshape(32, 8, 128)

    second = est_copies(1, cur)
    pl.when(has_right)(second[0].start)
    pl.when(has_left)(second[1].start)
    exchange(1, second, cur, lambda: None)
    rows_forward()
    acc[...] = jnp.zeros_like(acc)

    def view1(v, _):
        blur_and_ratio(1, v)
        return 0

    lax.fori_loop(0, views, view1, 0)

    lane = iota((8, 128), 1)
    s = [jnp.sum(stat[k], axis=1, keepdims=True) for k in range(3)]
    msg[...] = jnp.where(lane == 0, s[0], jnp.where(lane == 1, s[1], s[2]))

    def send_msg(d, _):
        msg_copy(d).start()
        return 0

    lax.fori_loop(1, n, send_msg, 0)

    def view2(v, _):
        adjoint_log(v)
        return 0

    lax.fori_loop(0, views, view2, 0)

    def take_msg(d, total):
        msg_copy(d).wait()
        return total + msgs[d]

    total = lax.fori_loop(1, n, take_msg, msg[...])
    valid = (iota((8, 128), 0) < views) & (lane < 3)
    logs = jnp.log(jnp.where(valid, total, 1.0)) * jnp.where(lane == 1, -2.0, 1.0)
    log_scale = jnp.sum(jnp.sum(logs, axis=1, keepdims=True), axis=0, keepdims=True)
    for t in range(2):
        out[:, 8 * t : 8 * t + 8, :] = cur[:, 8 * t : 8 * t + 8, :] * jnp.exp(
            (acc[t] + log_scale) * (1.0 / views)
        ).reshape(32, 8, 128)

    for copies in (first, second):
        for k in range(4):
            pl.when(sends[k])(copies[k].wait_send)

    def drain(v, _):
        pl.when(has_right)(raw_copy(v, 0).wait_send)
        pl.when(has_left)(raw_copy(v, 1).wait_send)
        return 0

    lax.fori_loop(0, views, drain, 0)


def per_device(estimate, raw_views, psf_taps):
    n = lax.axis_size("slab")
    views = raw_views.shape[0]
    vmem = pl.BlockSpec(memory_space=pltpu.VMEM)
    dma = pltpu.SemaphoreType.DMA
    return pl.pallas_call(
        lambda *refs: kernel(n, views, *refs),
        out_shape=jax.ShapeDtypeStruct(estimate.shape, F32),
        in_specs=[vmem] * 3,
        out_specs=vmem,
        scratch_shapes=[
            pltpu.VMEM((views, 8, 128), F32),
            pltpu.VMEM((views * 48, 256), BF16),
            pltpu.VMEM((views, 16, 144), BF16),
            pltpu.VMEM((2, views, 256, 256), BF16),
            pltpu.VMEM((2, views, 512, 256), BF16),
            pltpu.VMEM((ITERS, 4, 32, 16, 128), F32),
            pltpu.VMEM((2, views, 32, 16, 128), F32),
            pltpu.VMEM((32, 256, 128), BF16),
            pltpu.VMEM((views, 6, 256, 256), BF16),
            pltpu.VMEM((views, 32, 144, 128), BF16),
            pltpu.VMEM((2, 256, 256), BF16),
            pltpu.VMEM((2, 256, 128), F32),
            pltpu.VMEM((32, 16, 128), F32),
            pltpu.VMEM((3, 8, 128), F32),
            pltpu.VMEM((8, 128), F32),
            pltpu.VMEM((n, 8, 128), F32),
            dma((ITERS, 4)), dma((ITERS, 4)), dma((views, 2)), dma((views, 2)), dma((n,)), dma((n,)),
        ],
        compiler_params=pltpu.CompilerParams(
            collective_id=0, has_side_effects=True, vmem_limit_bytes=56 * 1024 * 1024
        ),
    )(estimate, raw_views, psf_taps)


def solution(mesh):
    placed = (P("blocks", "slab", None), P(None, "blocks", "slab", None), P())
    return jax.shard_map(
        per_device, mesh=mesh, in_specs=placed, out_specs=P("blocks", "slab", None), check_vma=False
    )
```

profile of v0, /device:TPU:0, one launch (start us, length us, event | category | flops | bytes accessed | tf_op | source)
XLA Modules:
  0.0 87.0 jit_solution(6888442422644083115)
XLA Ops:
  0.0 85.3 %shard_map.37 = f32[32,16,128]{2,1,0:T(8,128)} custom-call(f32[32,16,128]{2,1,0:T(8,128)} %refs_0_.1, f32[6,32,16,128]{3,2,1,0:T(8,128)} %refs_1_.1, f32[6,3,31]{2,1,0:T(4,128)} %refs_2_.1), custom_call_target="tpu_custom_call" | custom-call | tf_op jit(solution)/shard_map/pallas_call | solution.py:281
  85.3 1.7 %copy.5 = f32[32,16,128]{2,1,0:T(8,128)} copy(f32[32,16,128]{2,1,0:T(8,128)} %shard_map.37) | data formatting | bytes 524288
where the time goes:
time: 87.5 us; the launch traced here: 87 us
  Pallas kernels  85.3 us (97%)
  local copies, waits for them, and re-layouts  1.67 us (2%)
    pallas_call x1, Pallas kernels, per_device(): pl.pallas_call(lambda *refs: kernel(n, views, *refs), out_shape=jax.Shape...  85.3 us

commit v1 on v0

--- a/solution.py
+++ b/solution.py
@@ -125,11 +125,19 @@
         frame[:, 80 + 16 * b : 96 + 16 * b, :] = lo
         frame[:, 160 + 16 * b : 176 + 16 * b, :] = hi
 
-    def exchange(it, copies, source, meanwhile):
+    odd = lax.rem(me, 2) == 1
+
+    def pass_on(copies, k):
+        pl.when(recvs[k])(copies[k].wait_recv)
+        pl.when(sends[2 + k])(copies[2 + k].start)
+
+    def exchange(it, copies, source, early, meanwhile):
+        pl.when(odd)(lambda: pass_on(copies, 0))
+        pl.when(jnp.logical_not(odd))(lambda: pass_on(copies, 1))
+        early()
         put_block(2, source)
-        for k in (0, 1):
-            pl.when(recvs[k])(copies[k].wait_recv)
-            pl.when(sends[2 + k])(copies[2 + k].start)
+        pl.when(odd)(lambda: pass_on(copies, 1))
+        pl.when(jnp.logical_not(odd))(lambda: pass_on(copies, 0))
         meanwhile()
         put_block(1, halo.at[it, 0])
         put_block(3, halo.at[it, 1])
@@ -146,6 +154,7 @@
 
         lax.fori_loop(0, views, go, 0)
 
+    def build_all():
         def build(v, _):
             build_matrices(v, tap_pad, ay, ayt, wx, mz)
             return 0
@@ -204,7 +213,7 @@
     def msg_copy(d):
         return copy(msg, msgs.at[d], msg_send.at[d], msg_recv.at[d], lax.rem(me + d, n))
 
-    exchange(0, first, est, start_raw)
+    exchange(0, first, est, start_raw, build_all)
     rows_forward()
     acc[...] = jnp.zeros_like(acc)
 
@@ -222,7 +231,7 @@
     second = est_copies(1, cur)
     pl.when(has_right)(second[0].start)
     pl.when(has_left)(second[1].start)
-    exchange(1, second, cur, lambda: None)
+    exchange(1, second, cur, lambda: None, lambda: None)
     rows_forward()
     acc[...] = jnp.zeros_like(acc)
 

time: 87.5 us -> 83.7 us (0.957)
  Pallas kernels: 85.3 us -> 81.8 us
    pallas_call x1, Pallas kernels: 85.3 us -> 81.8 us  [per_device(): pl.pallas_call(lambda *refs: kernel(n, views, *refs), out_shape=jax.Shape...]
where the time goes in v1:
time: 83.7 us; the launch traced here: 83.5 us
  Pallas kernels  81.8 us (98%)
  local copies, waits for them, and re-layouts  1.67 us (2%)
    pallas_call x1, Pallas kernels, per_device(): pl.pallas_call(lambda *refs: kernel(n, views, *refs), out_shape=jax.Shape...  81.8 us

profile of v1, /device:TPU:0, one launch (start us, length us, event | category | flops | bytes accessed | tf_op | source)
XLA Modules:
  0.0 83.5 jit_solution(417799086654605021)
XLA Ops:
  0.0 81.8 %shard_map.37 = f32[32,16,128]{2,1,0:T(8,128)} custom-call(f32[32,16,128]{2,1,0:T(8,128)} %refs_0_.1, f32[6,32,16,128]{3,2,1,0:T(8,128)} %refs_1_.1, f32[6,3,31]{2,1,0:T(4,128)} %refs_2_.1), custom_call_target="tpu_custom_call" | custom-call | tf_op jit(solution)/shard_map/pallas_call | solution.py:290
  81.8 1.7 %copy.5 = f32[32,16,128]{2,1,0:T(8,128)} copy(f32[32,16,128]{2,1,0:T(8,128)} %shard_map.37) | data formatting | bytes 524288

commit v2 on v1

--- a/solution.py
+++ b/solution.py
@@ -93,8 +93,9 @@
     def est_copies(it, source):
         srcs = (source, source, halo.at[it, 0], halo.at[it, 1])
         tos = (right, left, right, left)
+        rows = (slice(None), slice(None), pl.ds(2, 14), pl.ds(0, 14))
         return [
-            copy(srcs[k], halo.at[it, k], est_send.at[it, k], est_recv.at[it, k], tos[k]) for k in range(4)
+            copy(srcs[k].at[:, rows[k]], halo.at[it, k, :, rows[k]], est_send.at[it, k], est_recv.at[it, k], tos[k]) for k in range(4)
         ]
 
     both = has_left & has_right
@@ -102,7 +103,10 @@
     recvs = (has_left, has_right, me > 1, me < n - 2)
 
     def raw_copy(v, k):
-        return copy(raw.at[v], raw_halo.at[k, v], raw_send.at[v, k], raw_recv.at[v, k], (right, left)[k])
+        rows = pl.ds(1 - k, 15)
+        return copy(
+            raw.at[v, :, rows], raw_halo.at[k, v, :, rows], raw_send.at[v, k], raw_recv.at[v, k], (right, left)[k]
+        )
 
     first = est_copies(0, est)
     pl.when(has_right)(first[0].start)
@@ -113,7 +117,11 @@
         tap_pad[v, 0:3, 0:31] = taps[v]
     stat[...] = jnp.zeros_like(stat)
     frame[:, 240:256, :] = jnp.zeros((32, 16, 128), BF16)
+    raw_halo[0, :, :, 0:1, :] = jnp.zeros((views, 32, 1, 128), F32)
+    raw_halo[1, :, :, 15:16, :] = jnp.zeros((views, 32, 1, 128), F32)
     for it in range(ITERS):
+        halo[it, 2, :, 0:2, :] = jnp.zeros((32, 2, 128), F32)
+        halo[it, 3, :, 14:16, :] = jnp.zeros((32, 2, 128), F32)
         for k, there in enumerate(recvs):
             @pl.when(jnp.logical_not(there))
             def _():
@@ -191,7 +199,8 @@
         ):
             value = block[...] / jnp.concatenate([blurred[2 * b], blurred[2 * b + 1]], 1)
             if there is not None:
-                value = jnp.where(there, value, 0.0)
+                row = iota((32, 16, 128), 1)
+                value = jnp.where(there & (row != (0 if b == 0 else 15)), value, 0.0)
             hi, lo = split(value)
             ratio3[v, :, 16 * b : 16 * b + 16, :] = hi
             ratio3[v, :, 48 + 16 * b : 64 + 16 * b, :] = lo

time: 83.7 us -> 81.5 us (0.974)
  Pallas kernels: 81.8 us -> 79.7 us
    pallas_call x1, Pallas kernels: 81.8 us -> 79.7 us  [per_device(): pl.pallas_call(lambda *refs: kernel(n, views, *refs), out_shape=jax.Shape...]
where the time goes in v2:
time: 81.5 us; the launch traced here: 81.4 us
  Pallas kernels  79.7 us (98%)
  local copies, waits for them, and re-layouts  1.67 us (2%)
    pallas_call x1, Pallas kernels, per_device(): pl.pallas_call(lambda *refs: kernel(n, views, *refs), out_shape=jax.Shape...  79.7 us
    unnamed x1, local copies, waits for them, and re-layouts  1.67 us

profile of v2, /device:TPU:0, one launch (start us, length us, event | category | flops | bytes accessed | tf_op | source)
XLA Modules:
  0.0 81.4 jit_solution(12718874609345789789)
XLA Ops:
  0.0 79.7 %shard_map.37 = f32[32,16,128]{2,1,0:T(8,128)} custom-call(f32[32,16,128]{2,1,0:T(8,128)} %refs_0_.1, f32[6,32,16,128]{3,2,1,0:T(8,128)} %refs_1_.1, f32[6,3,31]{2,1,0:T(4,128)} %refs_2_.1), custom_call_target="tpu_custom_call" | custom-call | tf_op jit(solution)/shard_map/pallas_call | solution.py:299
  79.7 1.7 %copy.5 = f32[32,16,128]{2,1,0:T(8,128)} copy(f32[32,16,128]{2,1,0:T(8,128)} %shard_map.37) | data formatting | bytes 524288

commit v3 on v2

--- a/solution.py
+++ b/solution.py
@@ -156,13 +156,20 @@
 
     def start_raw():
         def go(v, _):
-            pl.when(has_right)(raw_copy(v, 0).start)
-            pl.when(has_left)(raw_copy(v, 1).start)
+            pl.when(has_right & odd)(raw_copy(v, 0).start)
+            pl.when(has_left & jnp.logical_not(odd))(raw_copy(v, 1).start)
             return 0
 
         lax.fori_loop(0, views, go, 0)
 
     def build_all():
+        def go(v, _):
+            pl.when(has_right & jnp.logical_not(odd))(raw_copy(v, 0).start)
+            pl.when(has_left & odd)(raw_copy(v, 1).start)
+            return 0
+
+        lax.fori_loop(0, views, go, 0)
+
         def build(v, _):
             build_matrices(v, tap_pad, ay, ayt, wx, mz)
             return 0

time: 81.5 us -> 81.5 us (level)
  no operation moved by 1% of the time
where the time goes in v3:
time: 81.5 us; the launch traced here: 81.4 us
  Pallas kernels  79.7 us (98%)
  local copies, waits for them, and re-layouts  1.67 us (2%)
    pallas_call x1, Pallas kernels, per_device(): pl.pallas_call(lambda *refs: kernel(n, views, *refs), out_shape=jax.Shape...  79.7 us
    unnamed x1, local copies, waits for them, and re-layouts  1.67 us

profile of v3, /device:TPU:0, one launch (start us, length us, event | category | flops | bytes accessed | tf_op | source)
XLA Modules:
  0.0 81.4 jit_solution(3683816352887448765)
XLA Ops:
  0.0 79.7 %shard_map.37 = f32[32,16,128]{2,1,0:T(8,128)} custom-call(f32[32,16,128]{2,1,0:T(8,128)} %refs_0_.1, f32[6,32,16,128]{3,2,1,0:T(8,128)} %refs_1_.1, f32[6,3,31]{2,1,0:T(4,128)} %refs_2_.1), custom_call_target="tpu_custom_call" | custom-call | tf_op jit(solution)/shard_map/pallas_call | solution.py:306
  79.7 1.7 %copy.5 = f32[32,16,128]{2,1,0:T(8,128)} copy(f32[32,16,128]{2,1,0:T(8,128)} %shard_map.37) | data formatting | bytes 524288
